TPU v7x, 256 devices: a whole 4x4x8 slice. The times are simulated.
256 devices in a mesh: dp: 32 (over x_hi, z, core), grp: 8 (over y, x_lo).
Axes of the slice: x: 4 (x_hi: 2, x_lo: 2; x = x_hi * 2 + x_lo), y: 4, z: 8, core: 2. Of those that a mesh axis runs over, the one named last changes fastest.
Arguments:
- images: bfloat16 [16384, 1152], P(('dp', 'grp')), may hold values from -24 to 24
- texts: bfloat16 [16384, 1152], P(('dp', 'grp')), may hold values from -24 to 24
- log_scale: float32 [1], replicated, may hold values from 4 to 4.8
- bias: float32 [1], replicated, may hold values from -12 to -8
Outputs:
- image_grad: float32 [16384, 1152], P(('dp', 'grp'))
- text_grad: float32 [16384, 1152], P(('dp', 'grp'))
- stats: float32 [3], replicated
All inputs are finite; a program needn't handle non-finite values.
Results may differ from a plain program's by a relative error of at most 0.002.
The roundings to bfloat16 on the way count: a program that leaves them out, or rounds other values in their place, can miss the bound.
Values may be sent and summed in bfloat16 or wider, within the bound.
No kernel may reach another device: no remote copies, remote signals or barrier semaphores. Data moves between devices by JAX's collectives and lax.ppermute only.
A program may use at most 64 MiB of HBM per device.

v0:
```python
import jax
import jax.numpy as jnp
from jax import lax
from jax.sharding import PartitionSpec as P

EPS = 1e-06


def normalize(rows):
    values = rows.astype(jnp.float32)
    norms = jnp.sqrt(jnp.sum(values * values, axis=-1, keepdims=True) + EPS)
    return (values / norms, norms)


def project(direction, unit, norms):
    along = jnp.sum(direction * unit, axis=-1, keepdims=True)
    return (direction - unit * along) / norms


def on_device(images, texts, log_scale, bias):
    rows = images.shape[0]
    img_unit, img_norm = normalize(images)
    txt_unit, txt_norm = normalize(texts)
    img_low = img_unit.astype(jnp.bfloat16)
    txt_low = txt_unit.astype(jnp.bfloat16)
    scale = jnp.exp(log_scale[0])
    shift = bias[0]
    dp_index = lax.axis_index("dp")
    grp_index = lax.axis_index("grp")
    block_imgs = lax.all_gather(img_low, "grp", axis=0, tiled=True)
    img_count = block_imgs.shape[0]
    img_pos = lax.broadcasted_iota(jnp.int32, (img_count, 1), 0)
    piece = lax.all_gather(txt_low, "dp", axis=0, tiled=True)
    count = piece.shape[0]
    cosine = jnp.einsum("ie,je->ij", block_imgs, piece, preferred_element_type=jnp.float32)
    scaled = scale * cosine
    logits = scaled + shift
    local = lax.broadcasted_iota(jnp.int32, (1, count), 1) - dp_index * rows
    positive = (local >= 0) & (local < rows) & (img_pos == grp_index * rows + local)
    sign = jnp.where(positive, 1.0, -1.0).astype(jnp.float32)
    losses = jax.nn.softplus(-sign * logits)
    grad = jax.nn.sigmoid(logits) - positive.astype(jnp.float32)
    sums = jnp.stack([jnp.sum(losses), jnp.sum(grad * scaled), jnp.sum(grad)])
    grad_low, sums = (grad.astype(jnp.bfloat16), sums)
    img_acc = jnp.dot(grad_low, piece, preferred_element_type=jnp.float32)
    term = jnp.einsum("ij,ie->je", grad_low, block_imgs, preferred_element_type=jnp.float32)
    txt_acc = term
    img_acc, txt_acc, totals = (img_acc, txt_acc, sums)
    txt_part = lax.psum_scatter(txt_acc, "dp", scatter_dimension=0, tiled=True)
    img_part = lax.psum_scatter(img_acc, "grp", scatter_dimension=0, tiled=True)
    overall = lax.psum(totals, ("dp", "grp"))
    batch_rows = rows * lax.axis_size("dp") * lax.axis_size("grp")
    image_grad = project(scale * img_part, img_unit, img_norm)
    text_grad = project(scale * txt_part, txt_unit, txt_norm)
    return (image_grad, text_grad, overall / batch_rows)


def solution(mesh):
    in_specs = (P(("dp", "grp"), None), P(("dp", "grp"), None), P(), P())
    out_specs = (P(("dp", "grp"), None), P(("dp", "grp"), None), P())
    return jax.shard_map(
        on_device, mesh=mesh, in_specs=in_specs, out_specs=out_specs, check_vma=False
    )
```

profile of v0, /device:TPU:8, one launch (start us, length us, event | category | flops | bytes accessed | tf_op | source)
XLA Modules:
  0.0 395.3 jit_solution(9898853837945935118)
XLA Ops:
  7.2 0.0 all-gather.3.cloned.1.call-start
  7.2 1.0 fusion.6
  8.3 1.7 fusion.12
  9.9 0.0 all-gather.3.cloned.1.call-update
  10.0 0.0 all-gather.5.cloned.1.call-start
  10.0 1.0 fusion.7
  11.1 1.7 fusion.13
  12.8 0.0 all-gather.5.cloned.1.call-update
  12.8 0.0 reduce-scatter.3.cloned.1.call-start
  14.2 41.0 %all-gather.3.cloned.1.call-done = bf16[512,1152]{1,0:T(8,128)(2,1)} async-done(((bf16[64,1152]{1,0:T(8,128)(2,1)}), bf16[512,1152]{1,0:T(8,128)(2,1)}) %all-gather.3.cloned.1.call-update) | async-done | bytes 1179664 | tf_op jit(solution)/shard_map/all_gather | solution.py:30
  55.2 93.0 %all-gather.5.cloned.1.call-done = bf16[2048,1152]{1,0:T(8,128)(2,1)} async-done(((bf16[64,1152]{1,0:T(8,128)(2,1)}), bf16[2048,1152]{1,0:T(8,128)(2,1)}) %all-gather.5.cloned.1.call-update) | async-done | bytes 4718608 | tf_op jit(solution)/shard_map/all_gather | solution.py:33
  148.1 0.0 copy-start.2
  148.1 10.1 %fusion = (f32[]{:T(128)}, f32[]{:T(128)}, f32[]{:T(128)}, f32[512,2048]{1,0:T(8,128)S(1)}) fusion(s32[2048]{0:T(1024)S(1)} %fusion.8, f32[]{:T(128)} %bitcast.10, f32[]{:T(128)} %bitcast, pred[2048]{0:T(1024)(128)(4,1)S(1)} %fusion.11, bf16[512,1152]{1,0:T(8,128)(2,1)} %all-gather.3.cloned.1.call-done, bf16[2048,1152]{1,0:T(8,128)(2,1)} %all-gather.5.cloned.1.call-done), kind=kOutput, calls=%fused_computation.1 | convolution fusion | flops 2438987776 | bytes 10102804 | tf_op jit(solution)/shard_map/ie,je->ij/dot_general | solution.py:35
  158.3 0.0 copy-start.4
  158.3 2.1 copy-done.4
  160.3 0.0 copy-done.2
  160.3 5.4 %fusion.4 = f32[512,1152]{1,0:T(8,128)} fusion(bf16[2048,1152]{1,0:T(8,128)(2,1)S(1)} %copy-done.2, f32[512,2048]{1,0:T(8,128)S(1)} %get-tuple-element.6, s32[2048]{0:T(1024)S(1)} %fusion.8, f32[]{:T(128)} %bitcast.9, f32[]{:T(128)} %bitcast, pred[2048]{0:T(1024)(128)(4,1)S(1)} %fusion.11), kind=kOutput, calls=%fused_computation.8 | convolution fusion | flops 2426404864 | bytes 11282440 | tf_op jit(solution)/shard_map/dot_general | solution.py:45
  165.8 0.0 reduce-scatter.3.cloned.1.call-update
  165.8 0.0 reduce-scatter.5.cloned.1.call-start
  165.8 0.0 copy-done.3
  165.8 9.8 %fusion.2 = f32[2048,1152]{1,0:T(8,128)} fusion(bf16[512,1152]{1,0:T(8,128)(2,1)S(1)} %copy-done.3, f32[512,2048]{1,0:T(8,128)} %copy-done.4, s32[2048]{0:T(1024)S(1)} %fusion.8, f32[]{:T(128)} %bitcast.11, f32[]{:T(128)} %bitcast, pred[2048]{0:T(1024)(128)(4,1)S(1)} %fusion.11), kind=kOutput, calls=%fused_computation.6 | convolution fusion | flops 2426404864 | bytes 14821384 | tf_op jit(solution)/shard_map/ij,ie->je/dot_general | solution.py:46
  175.6 0.0 reduce-scatter.5.cloned.1.call-update
  175.7 2.0 pad_maximum_fusion
  177.6 75.7 %psum.7 = f32[3]{0:T(128)S(1)} all-reduce(f32[3]{0:T(128)S(1)} %pad_maximum_fusion), channel_id=1, replica_groups=mesh['dp'=32,'grp'=8] {'dp','grp'}, use_global_device_ids=true, to_apply=%region_9.10 | all-reduce | flops 3 | bytes 24 | tf_op jit(solution)/shard_map/psum | solution.py:51
  253.4 0.5 broadcast_multiply_fusion
  253.9 0.0 copy-done
  253.9 1.2 multiply_reduce_fusion.2
  255.1 1.8 subtract_divide_fusion.1
  256.9 128.8 %reduce-scatter.5.cloned.1.call-done = f32[64,1152]{1,0:T(8,128)} async-done(((f32[2048,1152]{1,0:T(8,128)}), f32[64,1152]{1,0:T(8,128)}) %reduce-scatter.5.cloned.1.call-update) | async-done | bytes 294928 | tf_op jit(solution)/shard_map/reduce_scatter | solution.py:49
  385.8 0.0 copy-done.1
  385.8 1.2 multiply_reduce_fusion.1
  387.0 1.8 subtract_divide_fusion
  (8 shorter events, 0.0 us)
Async XLA Ops:
  7.2 48.0 %all-gather.3.cloned.1.call-start = ((), (), s32[]{:S(2)}) async-start(), calls=%async_computation.2 | async-start | bytes 1327104 | tf_op jit(solution)/shard_map/all_gather | solution.py:30
  10.0 138.2 %all-gather.5.cloned.1.call-start = ((), (), s32[]{:S(2)}) async-start(), calls=%async_computation.3 | async-start | bytes 4866048 | tf_op jit(solution)/shard_map/all_gather | solution.py:33
  12.8 241.1 %reduce-scatter.3.cloned.1.call-start = ((), (), s32[]{:S(2)}) async-start(), calls=%async_computation.4 | async-start | bytes 2654208 | tf_op jit(solution)/shard_map/reduce_scatter | solution.py:50
  148.1 12.2 %copy-start.2 = (bf16[2048,1152]{1,0:T(8,128)(2,1)S(1)}, bf16[2048,1152]{1,0:T(8,128)(2,1)}, u32[]{:S(2)}) copy-start(bf16[2048,1152]{1,0:T(8,128)(2,1)} %all-gather.5.cloned.1.call-done) | copy-start | bytes 14155780
  158.3 2.1 copy-start.4
  160.3 5.5 %copy-start.3 = (bf16[512,1152]{1,0:T(8,128)(2,1)S(1)}, bf16[512,1152]{1,0:T(8,128)(2,1)}, u32[]{:S(2)}) copy-start(bf16[512,1152]{1,0:T(8,128)(2,1)} %all-gather.3.cloned.1.call-done) | copy-start | bytes 3538948
  165.8 220.0 %reduce-scatter.5.cloned.1.call-start = ((), (), s32[]{:S(2)}) async-start(), calls=%async_computation.5 | async-start | bytes 9732096 | tf_op jit(solution)/shard_map/reduce_scatter | solution.py:49
  175.6 78.3 %copy-start = (bf16[64,1152]{1,0:T(8,128)(2,1)S(1)}, bf16[64,1152]{1,0:T(8,128)(2,1)}, u32[]{:S(2)}) copy-start(bf16[64,1152]{1,0:T(8,128)(2,1)} %param.4) | copy-start | bytes 442372
  175.6 210.2 %copy-start.1 = (bf16[64,1152]{1,0:T(8,128)(2,1)S(1)}, bf16[64,1152]{1,0:T(8,128)(2,1)}, u32[]{:S(2)}) copy-start(bf16[64,1152]{1,0:T(8,128)(2,1)} %param.5) | copy-start | bytes 442372
Sparse Core Ops, SparseCore 0:
  10.4 44.7 all-gather.2
  58.5 89.5 all-gather.4
  165.9 55.6 reduce-scatter.2
  225.9 159.8 reduce-scatter.4
where the time goes:
time: 396 us; the launch traced here: 395 us
  waiting for transfers between devices  263 us (66%)
  blocking collectives  75.7 us (19%)
  matrix products  25.3 us (6%)
  between operations  15.2 us (4%)
  other arithmetic  14 us (4%)
    reduce_scatter x1, waiting for transfers between devices, on_device(): txt_part = lax.psum_scatter(txt_acc, 'dp', scatter_dimension=0, tiled=True)  129 us
    all_gather x1, waiting for transfers between devices, on_device(): piece = lax.all_gather(txt_low, 'dp', axis=0, tiled=True)  93 us
    psum x1, blocking collectives, on_device(): overall = lax.psum(totals, ('dp', 'grp'))  75.7 us
    all_gather x1, waiting for transfers between devices, on_device(): block_imgs = lax.all_gather(img_low, 'grp', axis=0, tiled=True)  41 us
    dot_general x1, matrix products, on_device(): jnp.einsum('ie,je->ij', block_imgs, piece, preferred_element_type=jnp.flo...  10.1 us
    dot_general x1, matrix products, on_device(): jnp.einsum('ij,ie->je', grad_low, block_imgs, preferred_element_type=jnp....  9.78 us
  transfers between devices with their start and end apart: 4, of which 3 were waited for; matrix products, arithmetic and copies ran while one was open for 5% of the time, Pallas kernels for 0%

commit v1 on v0

--- a/solution.py
+++ b/solution.py
@@ -2,6 +2,7 @@
 import jax.numpy as jnp
 from jax import lax
 from jax.sharding import PartitionSpec as P
+from jax.lax import all_to_all, axis_size
 
 EPS = 1e-06
 
@@ -30,7 +31,8 @@
     block_imgs = lax.all_gather(img_low, "grp", axis=0, tiled=True)
     img_count = block_imgs.shape[0]
     img_pos = lax.broadcasted_iota(jnp.int32, (img_count, 1), 0)
-    piece = lax.all_gather(txt_low, "dp", axis=0, tiled=True)
+    reply = jnp.stack(axis_size("dp") * [txt_low])
+    piece = jnp.concatenate(all_to_all(reply, axis_name="dp", split_axis=0, concat_axis=0), axis=0)
     count = piece.shape[0]
     cosine = jnp.einsum("ie,je->ij", block_imgs, piece, preferred_element_type=jnp.float32)
     scaled = scale * cosine

time: 396 us -> 383 us (0.967)
  waiting for transfers between devices: 263 us -> 236 us
  starting transfers between devices: 0.16 us -> 11.7 us
    all_gather x1 -> x0, waiting for transfers between devices: 93 us -> none  [on_device(): piece = lax.all_gather(txt_low, 'dp', axis=0, tiled=True)]
    all_to_all x0 -> x1, waiting for transfers between devices: none -> 49.2 us  [on_device(): all_to_all(reply, axis_name='dp', split_axis=0, concat_axis=0)]
    all_gather x1, waiting for transfers between devices: 41 us -> 56.5 us  [on_device(): block_imgs = lax.all_gather(img_low, 'grp', axis=0, tiled=True)]
    all_to_all x0 -> x1, starting transfers between devices: none -> 11.6 us  [on_device(): all_to_all(reply, axis_name='dp', split_axis=0, concat_axis=0)]
  transfers between devices with their start and end apart: 4 -> 4, of which waited for: 3 -> 3; matrix products, arithmetic and copies ran while one was open for 5% -> 4% of each run, Pallas kernels for 0% -> 0%
where the time goes in v1:
time: 383 us
  waiting for transfers between devices  236 us (62%)
  blocking collectives  75.6 us (20%)
  matrix products  27.6 us (7%)
  between operations  15.2 us (4%)
  starting transfers between devices  11.7 us (3%)
  other arithmetic  11.5 us (3%)
  local copies, waits for them, and re-layouts  4.9 us (1%)
    reduce_scatter x1, waiting for transfers between devices, on_device(): txt_part = lax.psum_scatter(txt_acc, 'dp', scatter_dimension=0, tiled=True)  130 us
    psum x1, blocking collectives, on_device(): overall = lax.psum(totals, ('dp', 'grp'))  75.6 us
    all_gather x1, waiting for transfers between devices, on_device(): block_imgs = lax.all_gather(img_low, 'grp', axis=0, tiled=True)  56.5 us
    all_to_all x1, waiting for transfers between devices, on_device(): all_to_all(reply, axis_name='dp', split_axis=0, concat_axis=0)  49.2 us
    all_to_all x1, starting transfers between devices, on_device(): all_to_all(reply, axis_name='dp', split_axis=0, concat_axis=0)  11.6 us
    dot_general x1, matrix products, on_device(): jnp.einsum('ie,je->ij', block_imgs, piece, preferred_element_type=jnp.flo...  10 us
    dot_general x1, matrix products, on_device(): jnp.einsum('ij,ie->je', grad_low, block_imgs, preferred_element_type=jnp....  9.78 us
    dot_general x1, matrix products, on_device(): img_acc = jnp.dot(grad_low, piece, preferred_element_type=jnp.float32)  7.85 us
  transfers between devices with their start and end apart: 4, of which 3 were waited for; matrix products, arithmetic and copies ran while one was open for 4% of the time, Pallas kernels for 0%

profile of v1, /device:TPU:8, one launch (start us, length us, event | category | flops | bytes accessed | tf_op | source)
XLA Modules:
  0.0 382.7 jit_solution(3272737590777594774)
XLA Ops:
  7.2 1.0 fusion.7
  8.2 1.0 fusion.13
  9.2 2.8 stack.10
  12.1 0.0 copy-start
  12.1 11.6 %all-to-all-start = ((bf16[32,64,1152]{2,1,0:T(8,128)(2,1)}), bf16[32,64,1152]{2,1,0:T(8,128)(2,1)}, u32[]{:S(2)}, u32[]{:S(2)}) async-start(bf16[32,64,1152]{2,1,0:T(8,128)(2,1)} %stack.10), calls=%async_computation | async-start | bytes 9437184 | tf_op jit(solution)/shard_map/all_to_all | solution.py:35
  23.6 0.0 all-gather.2.cloned.1.call-start
  23.7 0.0 copy-done
  23.7 0.1 fusion.6
  23.8 0.8 fusion.12
  24.6 0.0 all-gather.2.cloned.1.call-update
  24.6 0.0 reduce-scatter.3.cloned.1.call-start
  26.0 56.5 %all-gather.2.cloned.1.call-done = bf16[512,1152]{1,0:T(8,128)(2,1)} async-done(((bf16[64,1152]{1,0:T(8,128)(2,1)}), bf16[512,1152]{1,0:T(8,128)(2,1)}) %all-gather.2.cloned.1.call-update) | async-done | bytes 1179664 | tf_op jit(solution)/shard_map/all_gather | solution.py:31
  82.6 49.2 %all-to-all-done = bf16[32,64,1152]{2,1,0:T(8,128)(2,1)} async-done(((bf16[32,64,1152]{2,1,0:T(8,128)(2,1)}), bf16[32,64,1152]{2,1,0:T(8,128)(2,1)}, u32[]{:S(2)}, u32[]{:S(2)}) %all-to-all-start) | async-done | bytes 4718624 | tf_op jit(solution)/shard_map/all_to_all | solution.py:35
  131.8 10.0 %fusion = (f32[]{:T(128)}, f32[]{:T(128)}, f32[]{:T(128)}, f32[512,2048]{1,0:T(8,128)S(1)}) fusion(s32[2048]{0:T(1024)S(1)} %fusion.8, f32[]{:T(128)} %bitcast.11, f32[]{:T(128)} %bitcast, pred[2048]{0:T(1024)(128)(4,1)S(1)} %fusion.11, bf16[512,1152]{1,0:T(8,128)(2,1)} %all-gather.2.cloned.1.call-done, bf16[2048,1152]{1,0:T(8,128)(2,1)} %bitcast.1), kind=kOutput, calls=%fused_computation.1 | convolution fusion | flops 2438987776 | bytes 10102804 | tf_op jit(solution)/shard_map/ie,je->ij/dot_general | solution.py:37
  141.8 0.0 copy-start.3
  141.8 2.1 copy-done.3
  143.9 0.0 copy-start.2
  143.9 7.9 %fusion.4 = f32[512,1152]{1,0:T(8,128)} fusion(bf16[2048,1152]{1,0:T(8,128)(2,1)} %bitcast.1, f32[512,2048]{1,0:T(8,128)S(1)} %get-tuple-element.6, s32[2048]{0:T(1024)S(1)} %fusion.8, f32[]{:T(128)} %bitcast.10, f32[]{:T(128)} %bitcast, pred[2048]{0:T(1024)(128)(4,1)S(1)} %fusion.11), kind=kOutput, calls=%fused_computation.8 | convolution fusion | flops 2426404864 | bytes 11282440 | tf_op jit(solution)/shard_map/dot_general | solution.py:47
  151.7 0.0 reduce-scatter.3.cloned.1.call-update
  151.7 0.0 reduce-scatter.5.cloned.1.call-start
  151.8 0.0 copy-done.2
  151.8 9.8 %fusion.2 = f32[2048,1152]{1,0:T(8,128)} fusion(bf16[512,1152]{1,0:T(8,128)(2,1)S(1)} %copy-done.2, f32[512,2048]{1,0:T(8,128)} %copy-done.3, s32[2048]{0:T(1024)S(1)} %fusion.8, f32[]{:T(128)} %bitcast.12, f32[]{:T(128)} %bitcast, pred[2048]{0:T(1024)(128)(4,1)S(1)} %fusion.11), kind=kOutput, calls=%fused_computation.6 | convolution fusion | flops 2426404864 | bytes 14821384 | tf_op jit(solution)/shard_map/ij,ie->je/dot_general | solution.py:48
  161.6 0.0 reduce-scatter.5.cloned.1.call-update
  161.6 2.0 pad_maximum_fusion
  163.6 75.6 %psum.7 = f32[3]{0:T(128)S(1)} all-reduce(f32[3]{0:T(128)S(1)} %pad_maximum_fusion), channel_id=1, replica_groups=mesh['dp'=32,'grp'=8] {'dp','grp'}, use_global_device_ids=true, to_apply=%region_9.10 | all-reduce | flops 3 | bytes 24 | tf_op jit(solution)/shard_map/psum | solution.py:53
  239.2 0.5 broadcast_multiply_fusion
  239.7 1.2 multiply_reduce_fusion.2
  240.9 1.8 subtract_divide_fusion.1
  242.7 130.4 %reduce-scatter.5.cloned.1.call-done = f32[64,1152]{1,0:T(8,128)} async-done(((f32[2048,1152]{1,0:T(8,128)}), f32[64,1152]{1,0:T(8,128)}) %reduce-scatter.5.cloned.1.call-update) | async-done | bytes 294928 | tf_op jit(solution)/shard_map/reduce_scatter | solution.py:51
  373.2 0.0 copy-done.1
  373.2 1.2 multiply_reduce_fusion.1
  374.3 1.8 subtract_divide_fusion
  (6 shorter events, 0.0 us)
Async XLA Ops:
  12.1 11.6 %copy-start = (bf16[64,1152]{1,0:T(8,128)(2,1)S(1)}, bf16[64,1152]{1,0:T(8,128)(2,1)}, u32[]{:S(2)}) copy-start(bf16[64,1152]{1,0:T(8,128)(2,1)} %param.4) | copy-start | bytes 442372
  12.1 119.7 %all-to-all-start = ((bf16[32,64,1152]{2,1,0:T(8,128)(2,1)}), bf16[32,64,1152]{2,1,0:T(8,128)(2,1)}, u32[]{:S(2)}, u32[]{:S(2)}) async-start(bf16[32,64,1152]{2,1,0:T(8,128)(2,1)} %stack.10), calls=%async_computation | async-start | bytes 9437184 | tf_op jit(solution)/shard_map/all_to_all | solution.py:35
  23.6 58.9 %all-gather.2.cloned.1.call-start = ((), (), s32[]{:S(2)}) async-start(), calls=%async_computation.3 | async-start | bytes 1327104 | tf_op jit(solution)/shard_map/all_gather | solution.py:31
  24.6 215.1 %reduce-scatter.3.cloned.1.call-start = ((), (), s32[]{:S(2)}) async-start(), calls=%async_computation.4 | async-start | bytes 2654208 | tf_op jit(solution)/shard_map/reduce_scatter | solution.py:52
  141.8 2.1 copy-start.3
  143.9 7.9 %copy-start.2 = (bf16[512,1152]{1,0:T(8,128)(2,1)S(1)}, bf16[512,1152]{1,0:T(8,128)(2,1)}, u32[]{:S(2)}) copy-start(bf16[512,1152]{1,0:T(8,128)(2,1)} %all-gather.2.cloned.1.call-done) | copy-start | bytes 3538948
  151.7 221.4 %reduce-scatter.5.cloned.1.call-start = ((), (), s32[]{:S(2)}) async-start(), calls=%async_computation.5 | async-start | bytes 9732096 | tf_op jit(solution)/shard_map/reduce_scatter | solution.py:51
  161.6 211.6 %copy-start.1 = (bf16[64,1152]{1,0:T(8,128)(2,1)S(1)}, bf16[64,1152]{1,0:T(8,128)(2,1)}, u32[]{:S(2)}) copy-start(bf16[64,1152]{1,0:T(8,128)(2,1)} %param.5) | copy-start | bytes 442372
Sparse Core Ops, SparseCore 0:
  26.8 55.6 all-gather.1
  151.9 57.1 reduce-scatter.2
  213.5 159.6 reduce-scatter.4
